TPU v7x, 256 devices: a whole 4x4x8 slice. The times are simulated.
256 devices in a mesh: inp: 4 (over z_lo), out: 8 (over x, core), row: 8 (over y, z_hi).
Axes of the slice: x: 4, y: 4, z: 8 (z_hi: 2, z_lo: 4; z = z_hi * 4 + z_lo), core: 2. Of those that a mesh axis runs over, the one named last changes fastest.
Arguments:
- inputs: bfloat16 [4096, 5120], P('row', 'inp'), may hold values from -6 to 6
- grad_out: bfloat16 [4096, 5120], P('row', 'inp'), may hold values from -6 to 6
- gate_in: bfloat16 [4096, 10240], P('row', 'out'), may hold values from -6 to 6
- up_in: bfloat16 [4096, 10240], P('row', 'out'), may hold values from -6 to 6
- gate_weight: bfloat16 [5120, 10240], P('inp', ('out', 'row')), may hold values from -0.078125 to 0.078125
- up_weight: bfloat16 [5120, 10240], P('inp', ('out', 'row')), may hold values from -0.078125 to 0.078125
- down_weight: bfloat16 [10240, 5120], P(('out', 'row'), 'inp'), may hold values from -0.0625 to 0.0625
Outputs:
- grad_inputs: bfloat16 [4096, 5120], P('row', 'inp')
- grad_gate_w: float32 [5120, 10240], P('inp', ('out', 'row'))
- grad_up_w: float32 [5120, 10240], P('inp', ('out', 'row'))
- grad_down_w: float32 [10240, 5120], P(('out', 'row'), 'inp')
All inputs are finite; a program needn't handle non-finite values.
Results may differ from a plain program's by a relative error of at most 0.0049.
Values may be sent and summed in bfloat16 or wider, within the bound.
No kernel may reach another device: no remote copies, remote signals or barrier semaphores. Data moves between devices by JAX's collectives and lax.ppermute only.
A program may use at most 128 MiB of HBM per device.

v0:
```python
import jax
import jax.numpy as jnp
from jax import lax
from jax.sharding import Mesh, PartitionSpec as P

BF = jnp.bfloat16
F32 = jnp.float32


def after(a, *earlier):
    return lax.optimization_barrier((a,) + earlier)[0]


def send(a, axis, k, n=4):
    return lax.ppermute(a, axis, [(i, (i + k) % n) for i in range(n)])


def swap(a, axis):
    return send(a, axis, 1, 2)


def rows(a, at, n):
    return lax.dynamic_slice_in_dim(a, at * n, n, 0)


def nt(a, b):
    return lax.dot_general(a, b, (((1,), (1,)), ((), ())), preferred_element_type=F32)


def nn(a, b):
    return lax.dot_general(a, b, (((1,), (0,)), ((), ())), preferred_element_type=F32)


def tn(a, b):
    return lax.dot_general(a, b, (((0,), (0,)), ((), ())), preferred_element_type=F32)


def to_all(a, axis):
    return lax.all_to_all(jnp.tile(a, (4, 1)), axis, 0, 0, tiled=True)


def pick(a, at):
    return lax.dynamic_index_in_dim(a, at, 0, keepdims=False)


def place(parts, me):
    n = len(parts)
    slot = lax.broadcasted_iota(jnp.int32, (n, 1, 1), 0)
    got = parts[0][None]
    for k in range(1, n):
        got = jnp.where(slot == (me + k) % n, parts[k][None], got)
    return got


def place_xor(parts, me):
    slot = lax.broadcasted_iota(jnp.int32, (4, 1, 1), 0)
    got = parts[3][None]
    for k, part in zip((0, 2, 1), parts):
        got = jnp.where(slot == (me ^ k), part[None], got)
    return got


def from_all(a, axis):
    return [a] + [send(a, axis, -k) for k in (1, 2, 3)]


def fence(*values):
    return lax.optimization_barrier(values)


def exchange(a, k, axis="inp"):
    return lax.ppermute(a, axis, [(i, i ^ k) for i in range(4)])


def on_device(inputs, grad_out, gate_in, up_in, gate_weight, up_weight, down_weight):
    x, c, y, h = (lax.axis_index(name) for name in ("x", "core", "y", "h"))
    l = lax.axis_index("inp")
    tokens, width = inputs.shape
    block = down_weight.shape[0]
    piece = tokens // 8
    half = tokens // 2

    def in_order(part, swapped):
        part, swapped = part.reshape(half, width), swapped.reshape(half, width)
        return place([part, swapped], c).reshape(tokens, width)

    def half_of(a, which):
        a = a.T.reshape(4, 2, block, -1)
        return lax.dynamic_index_in_dim(a, which, 1, keepdims=False)

    both = jnp.concatenate(
        [rows(grad_out, 4 * c + x, piece), rows(inputs, 4 * c + x, piece)], 0
    )
    both = swap(both, "h")
    down = lax.all_gather(down_weight, "y", axis=0)
    ends = lax.cond(
        l == 3, lambda g, u: half_of(g, 1 - h), lambda g, u: half_of(u, 1 - h), gate_in, up_in
    )
    both, ends, gate_in, up_in, gate_weight, up_weight = fence(
        both, ends, gate_in, up_in, gate_weight, up_weight
    )
    g_piece, x_piece = both[:piece], both[piece:]
    ends = lax.ppermute(ends, ("inp", "h"), [(6, 1), (7, 0), (0, 7), (1, 6)])
    parts = from_all(g_piece, "x")
    both_w = jnp.concatenate([gate_weight.T, up_weight.T], 0)
    *parts, down, both_w, gate_in, up_in = fence(*parts, down, both_w, gate_in, up_in)

    weights = lax.all_gather(both_w, "y", axis=0, tiled=True)
    x_all = lax.all_gather(x_piece, ("x", "core"), axis=0, tiled=True)
    down_keep = jnp.concatenate([pick(down, l), pick(down, l ^ 2)], 0)
    down_give = jnp.concatenate([pick(down, l ^ 1), pick(down, l ^ 3)], 0)

    def terms_of(tok):
        return nt(down_keep, tok), nt(down_give, tok).astype(BF)

    def pair(keep, got):
        both = keep + got.astype(F32)
        return both[:block], both[block:].astype(BF)

    def whole(mine, got, others):
        return place_xor([mine, got, others[:block], others[block:]], l)

    mine_x = place(parts, x)
    grad_out_b = in_order(mine_x, swap(mine_x, "core"))
    keep_a, give_a = terms_of(grad_out)
    got_a = exchange(give_a, 1)
    near = lax.ppermute(ends, "inp", [(0, 1), (3, 2)])
    keep_b, give_b = terms_of(grad_out_b)
    mine_a, give_a = pair(keep_a, got_a)
    mine_a, give_a, near, keep_b, give_b, gate_in, up_in = fence(
        mine_a, give_a, near, keep_b, give_b, gate_in, up_in
    )

    got_a = exchange(give_a, 2)
    got_b = exchange(give_b, 1)
    far = lax.ppermute(near, "inp", [(1, 2), (2, 1)])
    gate_a, up_a = half_of(gate_in, h), half_of(up_in, h)
    mine_a = (mine_a + got_a.astype(F32)).astype(BF)
    mine_b, give_b = pair(keep_b, got_b)
    mine_a, mine_b, give_b, far, gate_a, up_a = fence(mine_a, mine_b, give_b, far, gate_a, up_a)

    got_a = exchange(mine_a, 2)
    got_b = exchange(give_b, 2)
    last = lax.ppermute(far, "inp", [(2, 3), (1, 0)])
    mine_b = (mine_b + got_b.astype(F32)).astype(BF)
    both_a = jnp.concatenate([mine_a, got_a], 0)
    both_a, mine_b, last, x_all = fence(both_a, mine_b, last, x_all)

    gate_b = jnp.where(l == 0, ends, jnp.where(l == 1, near, jnp.where(l == 2, far, last)))
    up_b = jnp.where(l == 3, ends, jnp.where(l == 2, near, jnp.where(l == 1, far, last)))
    others_a = exchange(both_a, 1)
    got_b = exchange(mine_b, 2)

    def gate_part(gate, up):
        gate, up = gate.astype(F32), up.astype(F32)
        logistic = jax.nn.sigmoid(gate)
        activated = gate * logistic
        return (activated * up).astype(BF).reshape(4 * block, tokens)

    def grad_part(gh, gate, up):
        gh, gate, up = gh.astype(F32), gate.astype(F32), up.astype(F32)
        logistic = jax.nn.sigmoid(gate)
        grad_gate = (gh * up * logistic * (1.0 + gate * (1.0 - logistic))).astype(BF)
        grad_up = (gh * (gate * logistic)).astype(BF)
        return jnp.stack([grad_gate, grad_up], 1).reshape(8 * block, tokens)

    def terms_y(left, right):
        n = left.shape[0] // 4
        terms = [nn(rows(left, (y + k) % 4, n), right) for k in range(4)]
        return terms[0], [a.astype(BF) for a in terms[1:]]

    def add(own, got):
        for a in got:
            own = own + a.astype(F32)
        return own

    both_b = jnp.concatenate([mine_b, got_b], 0)
    inputs_b = x_all.reshape(4, 2, piece, width).transpose(1, 0, 2, 3).reshape(tokens, width)
    hidden = jnp.concatenate([gate_part(gate_a, up_a), gate_part(gate_b, up_b)], 1)
    down_terms = nn(hidden, jnp.concatenate([grad_out, grad_out_b], 0)).astype(BF)
    others_a, both_b, inputs_b, down_terms = fence(others_a, both_b, inputs_b, down_terms)
    grad_down_w = lax.psum_scatter(down_terms, "y", scatter_dimension=0, tiled=True)

    def over_core(a):
        return (rows(a, c, half) + swap(rows(a, 1 - c, half), "core")).reshape(4, piece, width)

    others_b = exchange(both_b, 1)
    grads_a = grad_part(whole(both_a[:block], both_a[block:], others_a), gate_a, up_a)
    sum_a = tn(grads_a, weights)
    others_b, sum_a = fence(others_b, sum_a)

    grads_b = grad_part(whole(both_b[:block], both_b[block:], others_b), gate_b, up_b)
    core_a = over_core(sum_a)
    sum_b = tn(grads_b, weights)
    grads_a, grads_b, sum_b = fence(grads_a, grads_b, sum_b)
    core_b = over_core(sum_b)
    left = jnp.concatenate([grads_a, grads_b], 1)
    right = jnp.concatenate([inputs, inputs_b], 0)

    def term_w(k):
        return nn(rows(left, (y + k) % 4, 2 * block), right)

    cols = width // 2
    term_2 = term_w(2).astype(BF)
    up_half, down_half = send(term_2[:, :cols], "y", 1), send(term_2[:, cols:], "y", 3)
    term_1, term_3 = fence(term_w(1), term_w(3))
    core_a, core_b, term_1, term_3 = fence(core_a, core_b, term_1, term_3)

    none = jnp.zeros_like(up_half)
    term_1 = term_1 + jnp.concatenate([up_half, none], 1).astype(F32)
    term_3 = term_3 + jnp.concatenate([none, down_half], 1).astype(F32)
    got_1, got_3 = send(term_1.astype(BF), "y", 1), send(term_3.astype(BF), "y", 3)
    core = jnp.stack([core_a, core_b], 1)
    got = lax.all_to_all(core.astype(BF), "x", 0, 0, tiled=True).astype(F32)
    slot = lax.broadcasted_iota(jnp.int32, (4, 1, 1, 1), 0)
    summed = pick(core, x) + jnp.sum(jnp.where(slot == x, 0.0, got), axis=0)
    theirs = swap(summed[1].astype(BF), "h")
    theirs, got_1, got_3, grad_down_w = fence(theirs, got_1, got_3, grad_down_w)
    out_mine = to_all((summed[0] + theirs.astype(F32)).astype(BF), "x")
    grad_w = term_w(0) + got_1.astype(F32) + got_3.astype(F32)
    out_mine, grad_w = fence(out_mine, grad_w)
    grad_inputs = in_order(out_mine, swap(out_mine, "core"))
    return (grad_inputs, grad_w[:block].T, grad_w[block:].T, grad_down_w.astype(F32))


def solution(mesh):
    fine = Mesh(mesh.devices.reshape(4, 4, 2, 4, 2), ("inp", "x", "core", "y", "h"))
    out, row = ("x", "core"), ("y", "h")
    in_specs = (
        P(row, "inp"),
        P(row, "inp"),
        P(row, out),
        P(row, out),
        P("inp", out + row),
        P("inp", out + row),
        P(out + row, "inp"),
    )
    out_specs = (
        P(row, "inp"),
        P("inp", out + row),
        P("inp", out + row),
        P(out + row, "inp"),
    )
    return jax.shard_map(
        on_device, mesh=fine, in_specs=in_specs, out_specs=out_specs, check_vma=False
    )
```

profile of v0, /device:TPU:1, one launch (start us, length us, event | category | flops | bytes accessed | tf_op | source)
XLA Modules:
  0.0 230.0 jit_solution(6029336206248443139)
XLA Ops:
  9.7 7.7 %collective-permute-start = (bf16[128,1280]{1,0:T(8,128)(2,1)}, bf16[128,1280]{1,0:T(8,128)(2,1)}, u32[]{:S(2)}, u32[]{:S(2)}) collective-permute-start(bf16[128,1280]{1,0:T(8,128)(2,1)} %pad_maximum_fusion.12), channel_id=1, source_target_pairs={{0,1},{1,0},{2,3},{3,2},{4,5},{5,4},{6,7},{7,6},{8,9},{9,8},{10,11... | collective-permute-start | bytes 983048 | tf_op jit(solution)/shard_map/ppermute | solution.py:15
  19.2 6.5 %collective-permute-done = bf16[128,1280]{1,0:T(8,128)(2,1)} collective-permute-done((bf16[128,1280]{1,0:T(8,128)(2,1)}, bf16[128,1280]{1,0:T(8,128)(2,1)}, u32[]{:S(2)}, u32[]{:S(2)}) %collective-permute-start) | collective-permute-done | bytes 327712 | tf_op jit(solution)/shard_map/ppermute | solution.py:15
  29.4 2.5 %collective-permute-start.2 = (bf16[64,1280]{1,0:T(8,128)(2,1)S(1)}, bf16[64,1280]{1,0:T(8,128)(2,1)S(1)}, u32[]{:S(2)}, u32[]{:S(2)}) collective-permute-start(bf16[64,1280]{1,0:T(8,128)(2,1)S(1)} %get-tuple-element.81), channel_id=1, source_target_pairs={{0,32},{16,48},{32,0},{48,16},{1,33},{17,49},{33,1},{49,17},{2,34}... | collective-permute-start | bytes 491528 | tf_op jit(solution)/shard_map/ppermute | solution.py:15
  33.0 10.6 %collective-permute-start.5 = (bf16[4,160,512]{2,1,0:T(8,128)(2,1)S(1)}, bf16[4,160,512]{2,1,0:T(8,128)(2,1)}, u32[]{:S(2)}, u32[]{:S(2)}) collective-permute-start(bf16[4,160,512]{2,1,0:T(8,128)(2,1)S(1)} %get-tuple-element.162), channel_id=1, source_target_pairs={{192,1},{193,0},{0,193},{1,192},{194,3},{195,2},{2,195},{3,194},{1... | collective-permute-start | bytes 1966088 | tf_op jit(solution)/shard_map/ppermute | solution.py:103
  45.8 2.5 %dynamic-slice_bitcast_fusion.7 = (bf16[160,1280]{1,0:T(8,128)(2,1)}, bf16[160,1280]{1,0:T(8,128)(2,1)S(1)}, bf16[160,1280]{1,0:T(8,128)(2,1)S(1)}, bf16[160,1280]{1,0:T(8,128)(2,1)}) fusion(bf16[4,160,1280]{2,1,0:T(8,128)(2,1)} %bitcast.116, s32[]{:T(128)S(6)} %select_n.187, s32[]{:T(128)S(6)} %select_n.190, s32[]{:T(128)S(6)} %select_n.189, s32[]{:T(128)S(6)} %select_n.188), kind=kLoop, calls=%fused_computation.92 | loop fusion | bytes 3276816 | tf_op jit(solution)/shard_map/jit(dynamic_index_in_dim)/squeeze | solution.py:43
  50.7 2.2 select_select_fusion.4
  57.3 3.7 %collective-permute-start.6 = (bf16[4,160,512]{2,1,0:T(8,128)(2,1)}, bf16[4,160,512]{2,1,0:T(8,128)(2,1)}, u32[]{:S(2)}, u32[]{:S(2)}) collective-permute-start(bf16[4,160,512]{2,1,0:T(8,128)(2,1)} %collective-permute-done.5), channel_id=1, source_target_pairs={{0,64},{192,128},{1,65},{193,129},{2,66},{194,130},{3,67},{195,131... | collective-permute-start | bytes 1966088 | tf_op jit(solution)/shard_map/ppermute | solution.py:127
  67.1 7.3 %collective-permute-done.6 = bf16[4,160,512]{2,1,0:T(8,128)(2,1)} collective-permute-done((bf16[4,160,512]{2,1,0:T(8,128)(2,1)}, bf16[4,160,512]{2,1,0:T(8,128)(2,1)}, u32[]{:S(2)}, u32[]{:S(2)}) %collective-permute-start.6) | collective-permute-done | bytes 655392 | tf_op jit(solution)/shard_map/ppermute | solution.py:127
  74.3 4.1 %collective-permute-start.8 = (bf16[160,512]{1,0:T(8,128)(2,1)}, bf16[160,512]{1,0:T(8,128)(2,1)S(1)}, u32[]{:S(2)}, u32[]{:S(2)}) collective-permute-start(bf16[160,512]{1,0:T(8,128)(2,1)} %slice.104), channel_id=1, source_target_pairs={{0,128},{64,192},{128,0},{192,64},{1,129},{65,193},{129,1},{193,65... | collective-permute-start | bytes 491528 | tf_op jit(solution)/shard_map/ppermute | solution.py:72
  86.8 3.7 %collective-permute-done.9 = bf16[320,512]{1,0:T(8,128)(2,1)} collective-permute-done((bf16[320,512]{1,0:T(8,128)(2,1)}, bf16[320,512]{1,0:T(8,128)(2,1)}, u32[]{:S(2)}, u32[]{:S(2)}) %collective-permute-start.9) | collective-permute-done | bytes 327712 | tf_op jit(solution)/shard_map/ppermute | solution.py:72
  91.7 8.5 %collective-permute-start.12 = (bf16[160,512]{1,0:T(8,128)(2,1)S(1)}, bf16[160,512]{1,0:T(8,128)(2,1)S(1)}, u32[]{:S(2)}, u32[]{:S(2)}) collective-permute-start(bf16[160,512]{1,0:T(8,128)(2,1)S(1)} %slice.103), channel_id=1, source_target_pairs={{0,128},{64,192},{128,0},{192,64},{1,129},{65,193},{129,1},{193,65... | collective-permute-start | bytes 491528 | tf_op jit(solution)/shard_map/ppermute | solution.py:72
  102.8 11.6 %collective-permute-done.11 = bf16[160,512]{1,0:T(8,128)(2,1)S(1)} collective-permute-done((bf16[160,512]{1,0:T(8,128)(2,1)S(1)}, bf16[160,512]{1,0:T(8,128)(2,1)S(1)}, u32[]{:S(2)}, u32[]{:S(2)}) %collective-permute-start.11) | collective-permute-done | bytes 163872 | tf_op jit(solution)/shard_map/ppermute | solution.py:72
  115.2 7.7 %collective-permute-done.13 = bf16[4,160,512]{2,1,0:T(8,128)(2,1)S(1)} collective-permute-done((bf16[4,160,512]{2,1,0:T(8,128)(2,1)}, bf16[4,160,512]{2,1,0:T(8,128)(2,1)S(1)}, u32[]{:S(2)}, u32[]{:S(2)}) %collective-permute-start.13) | collective-permute-done | bytes 655392 | tf_op jit(solution)/shard_map/ppermute | solution.py:144
  125.3 3.0 %collective-permute-start.15 = (bf16[160,512]{1,0:T(8,128)(2,1)S(1)}, bf16[160,512]{1,0:T(8,128)(2,1)}, u32[]{:S(2)}, u32[]{:S(2)}) collective-permute-start(bf16[160,512]{1,0:T(8,128)(2,1)S(1)} %add_convert_fusion.2), channel_id=1, source_target_pairs={{0,128},{64,192},{128,0},{192,64},{1,129},{65,193},{129,1},{193,65... | collective-permute-start | bytes 491528 | tf_op jit(solution)/shard_map/ppermute | solution.py:72
  130.4 3.1 %fusion.6 = (bf16[4,160,512]{2,1,0:T(8,128)(2,1)S(1)}, bf16[4,160,512]{2,1,0:T(8,128)(2,1)S(1)}, bf16[4,160,512]{2,1,0:T(8,128)(2,1)}) fusion(bf16[4,160,512]{2,1,0:T(8,128)(2,1)} %collective-permute-done.5, bf16[4,160,512]{2,1,0:T(8,128)(2,1)} %collective-permute-done.6, bf16[4,160,512]{2,1,0:T(8,128)(2,1)} %collective-permute-done.10, ...), kind=kLoop, calls=%fused_computation.29 | loop fusion | flops 4587520 | bytes 4587524 | tf_op jit(solution)/shard_map/convert_element_type | solution.py:158
  133.4 3.1 %convolution_convert_fusion = bf16[640,1280]{1,0:T(8,128)(2,1)} fusion(bf16[512,1280]{1,0:T(8,128)(2,1)S(1)} %copy-done.7, bf16[512,1280]{1,0:T(8,128)(2,1)S(1)} %copy-done.29, bf16[640,512]{1,0:T(8,128)(2,1)S(1)} %bitcast.119, bf16[640,512]{1,0:T(8,128)(2,1)S(1)} %bitcast.118), kind=kOutput, calls=%fused_computation.2 | convolution fusion | flops 1686405120 | bytes 5570560 | tf_op jit(solution)/shard_map/dot_general | solution.py:31
  145.6 3.9 %fusion.61 = f32[512,1280]{1,0:T(8,128)S(1)} fusion(bf16[1280,512]{1,0:T(8,128)(2,1)S(1)} %bitcast.106, bf16[1280,1280]{1,0:T(8,128)(2,1)} %all-gather.7.cloned.1.call-done), kind=kOutput, calls=%fused_computation.136 | convolution fusion | flops 1677721600 | bytes 7208960 | tf_op jit(solution)/shard_map/dot_general | solution.py:35
  155.8 2.5 %collective-permute-start.17 = (f32[256,1280]{1,0:T(8,128)S(1)}, f32[256,1280]{1,0:T(8,128)S(1)}, u32[]{:S(2)}, u32[]{:S(2)}) collective-permute-start(f32[256,1280]{1,0:T(8,128)S(1)} %constant_dynamic-slice_fusion.1), channel_id=1, source_target_pairs={{0,8},{8,0},{1,9},{9,1},{2,10},{10,2},{3,11},{11,3},{4,12},{12,4},... | collective-permute-start | bytes 3932168 | tf_op jit(solution)/shard_map/ppermute | solution.py:15
  159.7 3.0 %collective-permute-start.22 = (bf16[320,640]{1,0:T(8,128)(2,1)S(1)}, bf16[320,640]{1,0:T(8,128)(2,1)}, u32[]{:S(2)}, u32[]{:S(2)}) collective-permute-start(bf16[320,640]{1,0:T(8,128)(2,1)S(1)} %get-tuple-element.144), channel_id=1, source_target_pairs={{0,6},{2,0},{4,2},{6,4},{1,7},{3,1},{5,3},{7,5},{8,14},{10,8},{12,... | collective-permute-start | bytes 1228808 | tf_op jit(solution)/shard_map/ppermute | solution.py:15
  162.7 2.2 fusion.35
  164.9 2.2 fusion.37
  168.6 4.3 %all-to-all-start = ((bf16[4,2,64,1280]{3,2,1,0:T(8,128)(2,1)}), bf16[4,2,64,1280]{3,2,1,0:T(8,128)(2,1)}, u32[]{:S(2)}, u32[]{:S(2)}) async-start(bf16[4,2,64,1280]{3,2,1,0:T(8,128)(2,1)} %fusion.1), calls=%async_computation | async-start | bytes 2621440 | tf_op jit(solution)/shard_map/all_to_all | solution.py:214
  172.9 3.6 %collective-permute-done.22 = bf16[320,640]{1,0:T(8,128)(2,1)} collective-permute-done((bf16[320,640]{1,0:T(8,128)(2,1)S(1)}, bf16[320,640]{1,0:T(8,128)(2,1)}, u32[]{:S(2)}, u32[]{:S(2)}) %collective-permute-start.22) | collective-permute-done | bytes 409632 | tf_op jit(solution)/shard_map/ppermute | solution.py:15
  176.6 2.5 %add_convert_fusion = bf16[320,1280]{1,0:T(8,128)(2,1)} fusion(f32[320,1280]{1,0:T(8,128)} %fusion.35, bf16[320,640]{1,0:T(8,128)(2,1)} %collective-permute-done.22), kind=kLoop, calls=%fused_computation.20 | loop fusion | flops 1228800 | bytes 2867200 | tf_op jit(solution)/shard_map/convert_element_type | solution.py:212
  179.1 2.4 %collective-permute-start.23 = (bf16[320,1280]{1,0:T(8,128)(2,1)}, bf16[320,1280]{1,0:T(8,128)(2,1)}, u32[]{:S(2)}, u32[]{:S(2)}) collective-permute-start(bf16[320,1280]{1,0:T(8,128)(2,1)} %add_convert_fusion), channel_id=1, source_target_pairs={{0,6},{2,0},{4,2},{6,4},{1,7},{3,1},{5,3},{7,5},{8,14},{10,8},{12,... | collective-permute-start | bytes 2457608 | tf_op jit(solution)/shard_map/ppermute | solution.py:15
  183.5 5.8 %all-to-all-done = bf16[4,2,64,1280]{3,2,1,0:T(8,128)(2,1)} async-done(((bf16[4,2,64,1280]{3,2,1,0:T(8,128)(2,1)}), bf16[4,2,64,1280]{3,2,1,0:T(8,128)(2,1)}, u32[]{:S(2)}, u32[]{:S(2)}) %all-to-all-start) | async-done | bytes 1310752 | tf_op jit(solution)/shard_map/all_to_all | solution.py:214
  191.3 6.9 %collective-permute-done.23 = bf16[320,1280]{1,0:T(8,128)(2,1)} collective-permute-done((bf16[320,1280]{1,0:T(8,128)(2,1)}, bf16[320,1280]{1,0:T(8,128)(2,1)}, u32[]{:S(2)}, u32[]{:S(2)}) %collective-permute-start.23) | collective-permute-done | bytes 819232 | tf_op jit(solution)/shard_map/ppermute | solution.py:15
  198.2 5.2 %collective-permute-done.21 = bf16[320,1280]{1,0:T(8,128)(2,1)} collective-permute-done((bf16[320,1280]{1,0:T(8,128)(2,1)}, bf16[320,1280]{1,0:T(8,128)(2,1)}, u32[]{:S(2)}, u32[]{:S(2)}) %collective-permute-start.21) | collective-permute-done | bytes 819232 | tf_op jit(solution)/shard_map/ppermute | solution.py:15
  204.3 3.8 %all-to-all-start.1 = ((bf16[4,64,1280]{2,1,0:T(8,128)(2,1)}), bf16[4,64,1280]{2,1,0:T(8,128)(2,1)S(1)}, u32[]{:S(2)}, u32[]{:S(2)}) async-start(bf16[4,64,1280]{2,1,0:T(8,128)(2,1)} %tile.2), calls=%async_computation.2 | async-start | bytes 1310720 | tf_op jit(solution)/shard_map/all_to_all | solution.py:39
  208.2 3.4 %fusion = f32[320,1280]{1,0:T(8,128)S(1)} fusion(bf16[1024,1280]{1,0:T(8,128)(2,1)} %constant_dynamic-update-slice_fusion.2, bf16[320,1280]{1,0:T(8,128)(2,1)} %collective-permute-done.23, bf16[320,1280]{1,0:T(8,128)(2,1)} %collective-permute-done.21, bf16[1280,1024]{1,0:T(8,128)(2,1)} %copy-done.10, s32[]{:T(128)S(6)} %select_n.229), kind=kOutput, calls=%fused_computation.7 | convolution fusion | flops 840499200 | bytes 6553604 | tf_op jit(solution)/shard_map/dot_general | solution.py:31
  211.6 4.6 %all-to-all-done.1 = bf16[4,64,1280]{2,1,0:T(8,128)(2,1)S(1)} async-done(((bf16[4,64,1280]{2,1,0:T(8,128)(2,1)}), bf16[4,64,1280]{2,1,0:T(8,128)(2,1)S(1)}, u32[]{:S(2)}, u32[]{:S(2)}) %all-to-all-start.1) | async-done | bytes 655392 | tf_op jit(solution)/shard_map/all_to_all | solution.py:39
  216.2 3.8 %collective-permute-start.24 = (bf16[256,1280]{1,0:T(8,128)(2,1)S(1)}, bf16[256,1280]{1,0:T(8,128)(2,1)S(1)}, u32[]{:S(2)}, u32[]{:S(2)}) collective-permute-start(bf16[256,1280]{1,0:T(8,128)(2,1)S(1)} %bitcast.114), channel_id=1, source_target_pairs={{0,8},{8,0},{1,9},{9,1},{2,10},{10,2},{3,11},{11,3},{4,12},{12,4},... | collective-permute-start | bytes 1966088 | tf_op jit(solution)/shard_map/ppermute | solution.py:15
  (179 shorter events, 69.0 us)
Async XLA Ops:
  7.2 38.6 %all-gather.9.cloned.1.call-start = ((), (), s32[]{:S(2)}) async-start(), calls=%async_computation.6 | async-start | bytes 2048000 | tf_op jit(solution)/shard_map/all_gather | solution.py:95
  7.9 107.3 %all-gather.5.cloned.1.call-start = ((), (), s32[]{:S(2)}) async-start(), calls=%async_computation.3 | async-start | bytes 1474560 | tf_op jit(solution)/shard_map/all_gather | solution.py:109
  9.7 15.9 %collective-permute-start = (bf16[128,1280]{1,0:T(8,128)(2,1)}, bf16[128,1280]{1,0:T(8,128)(2,1)}, u32[]{:S(2)}, u32[]{:S(2)}) collective-permute-start(bf16[128,1280]{1,0:T(8,128)(2,1)} %pad_maximum_fusion.12), channel_id=1, source_target_pairs={{0,1},{1,0},{2,3},{3,2},{4,5},{5,4},{6,7},{7,6},{8,9},{9,8},{10,11... | collective-permute-start | bytes 983048 | tf_op jit(solution)/shard_map/ppermute | solution.py:15
  27.4 118.2 %all-gather.7.cloned.1.call-start = ((), (), s32[]{:S(2)}) async-start(), calls=%async_computation.4 | async-start | bytes 4096000 | tf_op jit(solution)/shard_map/all_gather | solution.py:108
  27.6 18.1 %collective-permute-start.3 = (bf16[64,1280]{1,0:T(8,128)(2,1)S(1)}, bf16[64,1280]{1,0:T(8,128)(2,1)S(1)}, u32[]{:S(2)}, u32[]{:S(2)}) collective-permute-start(bf16[64,1280]{1,0:T(8,128)(2,1)S(1)} %get-tuple-element.81), channel_id=1, source_target_pairs={{0,16},{16,32},{32,48},{48,0},{1,17},{17,33},{33,49},{49,1},{2,18}... | collective-permute-start | bytes 491528 | tf_op jit(solution)/shard_map/ppermute | solution.py:15
  29.4 16.3 %collective-permute-start.2 = (bf16[64,1280]{1,0:T(8,128)(2,1)S(1)}, bf16[64,1280]{1,0:T(8,128)(2,1)S(1)}, u32[]{:S(2)}, u32[]{:S(2)}) collective-permute-start(bf16[64,1280]{1,0:T(8,128)(2,1)S(1)} %get-tuple-element.81), channel_id=1, source_target_pairs={{0,32},{16,48},{32,0},{48,16},{1,33},{17,49},{33,1},{49,17},{2,34}... | collective-permute-start | bytes 491528 | tf_op jit(solution)/shard_map/ppermute | solution.py:15
  31.8 13.9 %collective-permute-start.1 = (bf16[64,1280]{1,0:T(8,128)(2,1)S(1)}, bf16[64,1280]{1,0:T(8,128)(2,1)S(1)}, u32[]{:S(2)}, u32[]{:S(2)}) collective-permute-start(bf16[64,1280]{1,0:T(8,128)(2,1)S(1)} %get-tuple-element.81), channel_id=1, source_target_pairs={{0,48},{16,0},{32,16},{48,32},{1,49},{17,1},{33,17},{49,33},{2,50}... | collective-permute-start | bytes 491528 | tf_op jit(solution)/shard_map/ppermute | solution.py:15
  33.0 24.3 %collective-permute-start.5 = (bf16[4,160,512]{2,1,0:T(8,128)(2,1)S(1)}, bf16[4,160,512]{2,1,0:T(8,128)(2,1)}, u32[]{:S(2)}, u32[]{:S(2)}) collective-permute-start(bf16[4,160,512]{2,1,0:T(8,128)(2,1)S(1)} %get-tuple-element.162), channel_id=1, source_target_pairs={{192,1},{193,0},{0,193},{1,192},{194,3},{195,2},{2,195},{3,194},{1... | collective-permute-start | bytes 1966088 | tf_op jit(solution)/shard_map/ppermute | solution.py:103
  50.6 10.6 %collective-permute-start.4 = (bf16[320,512]{1,0:T(8,128)(2,1)}, bf16[320,512]{1,0:T(8,128)(2,1)}, u32[]{:S(2)}, u32[]{:S(2)}) collective-permute-start(bf16[320,512]{1,0:T(8,128)(2,1)} %convolution_convert_fusion.3), channel_id=1, source_target_pairs={{0,64},{64,0},{128,192},{192,128},{1,65},{65,1},{129,193},{193,129... | collective-permute-start | bytes 983048 | tf_op jit(solution)/shard_map/ppermute | solution.py:72
  50.7 140.6 %reduce-scatter.2.cloned.1.call-start = ((), (), s32[]{:S(2)}) async-start(), calls=%async_computation.5 | async-start | bytes 2048000 | tf_op jit(solution)/shard_map/reduce_scatter | solution.py:182
  52.9 10.8 %collective-permute-start.7 = (bf16[4,64,1280]{2,1,0:T(8,128)(2,1)}, bf16[4,64,1280]{2,1,0:T(8,128)(2,1)}, u32[]{:S(2)}, u32[]{:S(2)}) collective-permute-start(bf16[4,64,1280]{2,1,0:T(8,128)(2,1)} %select_select_fusion.4), channel_id=1, source_target_pairs={{0,8},{8,0},{1,9},{9,1},{2,10},{10,2},{3,11},{11,3},{4,12},{12,4},... | collective-permute-start | bytes 1966088 | tf_op jit(solution)/shard_map/ppermute | solution.py:15
  57.3 17.0 %collective-permute-start.6 = (bf16[4,160,512]{2,1,0:T(8,128)(2,1)}, bf16[4,160,512]{2,1,0:T(8,128)(2,1)}, u32[]{:S(2)}, u32[]{:S(2)}) collective-permute-start(bf16[4,160,512]{2,1,0:T(8,128)(2,1)} %collective-permute-done.5), channel_id=1, source_target_pairs={{0,64},{192,128},{1,65},{193,129},{2,66},{194,130},{3,67},{195,131... | collective-permute-start | bytes 1966088 | tf_op jit(solution)/shard_map/ppermute | solution.py:127
  74.3 12.4 %collective-permute-start.8 = (bf16[160,512]{1,0:T(8,128)(2,1)}, bf16[160,512]{1,0:T(8,128)(2,1)S(1)}, u32[]{:S(2)}, u32[]{:S(2)}) collective-permute-start(bf16[160,512]{1,0:T(8,128)(2,1)} %slice.104), channel_id=1, source_target_pairs={{0,128},{64,192},{128,0},{192,64},{1,129},{65,193},{129,1},{193,65... | collective-permute-start | bytes 491528 | tf_op jit(solution)/shard_map/ppermute | solution.py:72
  78.5 12.1 %collective-permute-start.9 = (bf16[320,512]{1,0:T(8,128)(2,1)}, bf16[320,512]{1,0:T(8,128)(2,1)}, u32[]{:S(2)}, u32[]{:S(2)}) collective-permute-start(bf16[320,512]{1,0:T(8,128)(2,1)} %convolution_convert_fusion.2), channel_id=1, source_target_pairs={{0,64},{64,0},{128,192},{192,128},{1,65},{65,1},{129,193},{193,129... | collective-permute-start | bytes 983048 | tf_op jit(solution)/shard_map/ppermute | solution.py:72
  78.5 13.2 %collective-permute-start.10 = (bf16[4,160,512]{2,1,0:T(8,128)(2,1)}, bf16[4,160,512]{2,1,0:T(8,128)(2,1)}, u32[]{:S(2)}, u32[]{:S(2)}) collective-permute-start(bf16[4,160,512]{2,1,0:T(8,128)(2,1)} %collective-permute-done.6), channel_id=1, source_target_pairs={{64,128},{128,64},{65,129},{129,65},{66,130},{130,66},{67,131},{13... | collective-permute-start | bytes 1966088 | tf_op jit(solution)/shard_map/ppermute | solution.py:136
  91.7 23.5 %collective-permute-start.12 = (bf16[160,512]{1,0:T(8,128)(2,1)S(1)}, bf16[160,512]{1,0:T(8,128)(2,1)S(1)}, u32[]{:S(2)}, u32[]{:S(2)}) collective-permute-start(bf16[160,512]{1,0:T(8,128)(2,1)S(1)} %slice.103), channel_id=1, source_target_pairs={{0,128},{64,192},{128,0},{192,64},{1,129},{65,193},{129,1},{193,65... | collective-permute-start | bytes 491528 | tf_op jit(solution)/shard_map/ppermute | solution.py:72
  100.2 14.2 %collective-permute-start.11 = (bf16[160,512]{1,0:T(8,128)(2,1)S(1)}, bf16[160,512]{1,0:T(8,128)(2,1)S(1)}, u32[]{:S(2)}, u32[]{:S(2)}) collective-permute-start(bf16[160,512]{1,0:T(8,128)(2,1)S(1)} %add_convert_fusion.3), channel_id=1, source_target_pairs={{0,128},{64,192},{128,0},{192,64},{1,129},{65,193},{129,1},{193,65... | collective-permute-start | bytes 491528 | tf_op jit(solution)/shard_map/ppermute | solution.py:72
  100.2 22.7 %collective-permute-start.13 = (bf16[4,160,512]{2,1,0:T(8,128)(2,1)}, bf16[4,160,512]{2,1,0:T(8,128)(2,1)S(1)}, u32[]{:S(2)}, u32[]{:S(2)}) collective-permute-start(bf16[4,160,512]{2,1,0:T(8,128)(2,1)} %collective-permute-done.10), channel_id=1, source_target_pairs={{128,192},{64,0},{129,193},{65,1},{130,194},{66,2},{131,195},{67,3... | collective-permute-start | bytes 1966088 | tf_op jit(solution)/shard_map/ppermute | solution.py:144
  125.3 12.3 %collective-permute-start.15 = (bf16[160,512]{1,0:T(8,128)(2,1)S(1)}, bf16[160,512]{1,0:T(8,128)(2,1)}, u32[]{:S(2)}, u32[]{:S(2)}) collective-permute-start(bf16[160,512]{1,0:T(8,128)(2,1)S(1)} %add_convert_fusion.2), channel_id=1, source_target_pairs={{0,128},{64,192},{128,0},{192,64},{1,129},{65,193},{129,1},{193,65... | collective-permute-start | bytes 491528 | tf_op jit(solution)/shard_map/ppermute | solution.py:72
  128.3 11.0 %collective-permute-start.14 = (bf16[320,512]{1,0:T(8,128)(2,1)}, bf16[320,512]{1,0:T(8,128)(2,1)}, u32[]{:S(2)}, u32[]{:S(2)}) collective-permute-start(bf16[320,512]{1,0:T(8,128)(2,1)} %pad_maximum_fusion.13), channel_id=1, source_target_pairs={{0,64},{64,0},{128,192},{192,128},{1,65},{65,1},{129,193},{193,129... | collective-permute-start | bytes 983048 | tf_op jit(solution)/shard_map/ppermute | solution.py:72
  141.4 8.1 %collective-permute-start.16 = (bf16[320,512]{1,0:T(8,128)(2,1)}, bf16[320,512]{1,0:T(8,128)(2,1)}, u32[]{:S(2)}, u32[]{:S(2)}) collective-permute-start(bf16[320,512]{1,0:T(8,128)(2,1)} %pad_maximum_fusion.14), channel_id=1, source_target_pairs={{0,64},{64,0},{128,192},{192,128},{1,65},{65,1},{129,193},{193,129... | collective-permute-start | bytes 983048 | tf_op jit(solution)/shard_map/ppermute | solution.py:72
  155.8 11.3 %collective-permute-start.17 = (f32[256,1280]{1,0:T(8,128)S(1)}, f32[256,1280]{1,0:T(8,128)S(1)}, u32[]{:S(2)}, u32[]{:S(2)}) collective-permute-start(f32[256,1280]{1,0:T(8,128)S(1)} %constant_dynamic-slice_fusion.1), channel_id=1, source_target_pairs={{0,8},{8,0},{1,9},{9,1},{2,10},{10,2},{3,11},{11,3},{4,12},{12,4},... | collective-permute-start | bytes 3932168 | tf_op jit(solution)/shard_map/ppermute | solution.py:15
  158.3 8.9 %collective-permute-start.18 = (f32[256,1280]{1,0:T(8,128)S(1)}, f32[256,1280]{1,0:T(8,128)S(1)}, u32[]{:S(2)}, u32[]{:S(2)}) collective-permute-start(f32[256,1280]{1,0:T(8,128)S(1)} %constant_dynamic-slice_fusion), channel_id=1, source_target_pairs={{0,8},{8,0},{1,9},{9,1},{2,10},{10,2},{3,11},{11,3},{4,12},{12,4},... | collective-permute-start | bytes 3932168 | tf_op jit(solution)/shard_map/ppermute | solution.py:15
  159.7 16.8 %collective-permute-start.22 = (bf16[320,640]{1,0:T(8,128)(2,1)S(1)}, bf16[320,640]{1,0:T(8,128)(2,1)}, u32[]{:S(2)}, u32[]{:S(2)}) collective-permute-start(bf16[320,640]{1,0:T(8,128)(2,1)S(1)} %get-tuple-element.144), channel_id=1, source_target_pairs={{0,6},{2,0},{4,2},{6,4},{1,7},{3,1},{5,3},{7,5},{8,14},{10,8},{12,... | collective-permute-start | bytes 1228808 | tf_op jit(solution)/shard_map/ppermute | solution.py:15
  162.7 18.8 %collective-permute-start.20 = (bf16[320,640]{1,0:T(8,128)(2,1)S(1)}, bf16[320,640]{1,0:T(8,128)(2,1)}, u32[]{:S(2)}, u32[]{:S(2)}) collective-permute-start(bf16[320,640]{1,0:T(8,128)(2,1)S(1)} %get-tuple-element.145), channel_id=1, source_target_pairs={{0,2},{2,4},{4,6},{6,0},{1,3},{3,5},{5,7},{7,1},{8,10},{10,12},{12... | collective-permute-start | bytes 1228808 | tf_op jit(solution)/shard_map/ppermute | solution.py:15
  168.6 20.7 %all-to-all-start = ((bf16[4,2,64,1280]{3,2,1,0:T(8,128)(2,1)}), bf16[4,2,64,1280]{3,2,1,0:T(8,128)(2,1)}, u32[]{:S(2)}, u32[]{:S(2)}) async-start(bf16[4,2,64,1280]{3,2,1,0:T(8,128)(2,1)} %fusion.1), calls=%async_computation | async-start | bytes 2621440 | tf_op jit(solution)/shard_map/all_to_all | solution.py:214
  179.1 19.2 %collective-permute-start.23 = (bf16[320,1280]{1,0:T(8,128)(2,1)}, bf16[320,1280]{1,0:T(8,128)(2,1)}, u32[]{:S(2)}, u32[]{:S(2)}) collective-permute-start(bf16[320,1280]{1,0:T(8,128)(2,1)} %add_convert_fusion), channel_id=1, source_target_pairs={{0,6},{2,0},{4,2},{6,4},{1,7},{3,1},{5,3},{7,5},{8,14},{10,8},{12,... | collective-permute-start | bytes 2457608 | tf_op jit(solution)/shard_map/ppermute | solution.py:15
  183.5 19.9 %collective-permute-start.21 = (bf16[320,1280]{1,0:T(8,128)(2,1)}, bf16[320,1280]{1,0:T(8,128)(2,1)}, u32[]{:S(2)}, u32[]{:S(2)}) collective-permute-start(bf16[320,1280]{1,0:T(8,128)(2,1)} %add_convert_fusion.1), channel_id=1, source_target_pairs={{0,2},{2,4},{4,6},{6,0},{1,3},{3,5},{5,7},{7,1},{8,10},{10,12},{12... | collective-permute-start | bytes 2457608 | tf_op jit(solution)/shard_map/ppermute | solution.py:15
  191.2 12.2 %collective-permute-start.19 = (bf16[64,1280]{1,0:T(8,128)(2,1)S(1)}, bf16[64,1280]{1,0:T(8,128)(2,1)S(1)}, u32[]{:S(2)}, u32[]{:S(2)}) collective-permute-start(bf16[64,1280]{1,0:T(8,128)(2,1)S(1)} %fusion.45), channel_id=1, source_target_pairs={{0,1},{1,0},{2,3},{3,2},{4,5},{5,4},{6,7},{7,6},{8,9},{9,8},{10,11... | collective-permute-start | bytes 491528 | tf_op jit(solution)/shard_map/ppermute | solution.py:15
  204.3 11.9 %all-to-all-start.1 = ((bf16[4,64,1280]{2,1,0:T(8,128)(2,1)}), bf16[4,64,1280]{2,1,0:T(8,128)(2,1)S(1)}, u32[]{:S(2)}, u32[]{:S(2)}) async-start(bf16[4,64,1280]{2,1,0:T(8,128)(2,1)} %tile.2), calls=%async_computation.2 | async-start | bytes 1310720 | tf_op jit(solution)/shard_map/all_to_all | solution.py:39
  208.2 11.8 %copy-start.20 = (bf16[160,1280]{1,0:T(8,128)(2,1)S(1)}, bf16[160,1280]{1,0:T(8,128)(2,1)}, u32[]{:S(2)}) copy-start(bf16[160,1280]{1,0:T(8,128)(2,1)} %reduce-scatter.2.cloned.1.call-done) | copy-start | bytes 1228804
  216.2 6.0 %collective-permute-start.24 = (bf16[256,1280]{1,0:T(8,128)(2,1)S(1)}, bf16[256,1280]{1,0:T(8,128)(2,1)S(1)}, u32[]{:S(2)}, u32[]{:S(2)}) collective-permute-start(bf16[256,1280]{1,0:T(8,128)(2,1)S(1)} %bitcast.114), channel_id=1, source_target_pairs={{0,8},{8,0},{1,9},{9,1},{2,10},{10,2},{3,11},{11,3},{4,12},{12,4},... | collective-permute-start | bytes 1966088 | tf_op jit(solution)/shard_map/ppermute | solution.py:15
  (31 other events, 132.6 us)
Sparse Core Ops, SparseCore 0:
  9.8 33.4 all-gather.8
  45.1 26.9 all-gather.4
  74.5 42.7 all-gather.6
  144.5 28.9 reduce-scatter.1
where the time goes:
time: 231 us; the launch traced here: 230 us
  starting transfers between devices  71.3 us (31%)
  waiting for transfers between devices  65.7 us (28%)
  local copies, waits for them, and re-layouts  29.1 us (13%)
  other arithmetic  26.7 us (12%)
  matrix products  22.8 us (10%)
  between operations  14.5 us (6%)
    ppermute x13, starting transfers between devices, send(): return lax.ppermute(a, axis, [(i, (i + k) % n) for i in range(n)])  26.8 us
    ppermute x13, waiting for transfers between devices, send(): return lax.ppermute(a, axis, [(i, (i + k) % n) for i in range(n)])  22.3 us
    ppermute x8, starting transfers between devices, exchange(): return lax.ppermute(a, axis, [(i, i ^ k) for i in range(4)])  19 us
    ppermute x8, waiting for transfers between devices, exchange(): return lax.ppermute(a, axis, [(i, i ^ k) for i in range(4)])  16.5 us
    dot_general x5, matrix products, nn(): lax.dot_general(a, b, (((1,), (0,)), ((), ())), preferred_element_type=F32)  12 us
    ppermute x1, starting transfers between devices, on_device(): ends = lax.ppermute(ends, ('inp', 'h'), [(6, 1), (7, 0), (0, 7), (1, 6)])  10.6 us
    ppermute x1, waiting for transfers between devices, on_device(): last = lax.ppermute(far, 'inp', [(2, 3), (1, 0)])  7.7 us
    ppermute x1, waiting for transfers between devices, on_device(): near = lax.ppermute(ends, 'inp', [(0, 1), (3, 2)])  7.26 us
  transfers between devices with their start and end apart: 31, of which 12 were waited for; matrix products, arithmetic and copies ran while one was open for 32% of the time, Pallas kernels for 0%

commit v1 on v0

--- a/solution.py
+++ b/solution.py
@@ -106,7 +106,7 @@
     *parts, down, both_w, gate_in, up_in = fence(*parts, down, both_w, gate_in, up_in)
 
     weights = lax.all_gather(both_w, "y", axis=0, tiled=True)
-    x_all = lax.all_gather(x_piece, ("x", "core"), axis=0, tiled=True)
+    inputs_b = lax.all_gather(x_piece, ("core", "x"), axis=0, tiled=True)
     down_keep = jnp.concatenate([pick(down, l), pick(down, l ^ 2)], 0)
     down_give = jnp.concatenate([pick(down, l ^ 1), pick(down, l ^ 3)], 0)
 
@@ -144,7 +144,7 @@
     last = lax.ppermute(far, "inp", [(2, 3), (1, 0)])
     mine_b = (mine_b + got_b.astype(F32)).astype(BF)
     both_a = jnp.concatenate([mine_a, got_a], 0)
-    both_a, mine_b, last, x_all = fence(both_a, mine_b, last, x_all)
+    both_a, mine_b, last, inputs_b = fence(both_a, mine_b, last, inputs_b)
 
     gate_b = jnp.where(l == 0, ends, jnp.where(l == 1, near, jnp.where(l == 2, far, last)))
     up_b = jnp.where(l == 3, ends, jnp.where(l == 2, near, jnp.where(l == 1, far, last)))
@@ -175,10 +175,9 @@
         return own
 
     both_b = jnp.concatenate([mine_b, got_b], 0)
-    inputs_b = x_all.reshape(4, 2, piece, width).transpose(1, 0, 2, 3).reshape(tokens, width)
     hidden = jnp.concatenate([gate_part(gate_a, up_a), gate_part(gate_b, up_b)], 1)
     down_terms = nn(hidden, jnp.concatenate([grad_out, grad_out_b], 0)).astype(BF)
-    others_a, both_b, inputs_b, down_terms = fence(others_a, both_b, inputs_b, down_terms)
+    others_a, both_b, down_terms = fence(others_a, both_b, down_terms)
     grad_down_w = lax.psum_scatter(down_terms, "y", scatter_dimension=0, tiled=True)
 
     def over_core(a):
@@ -203,8 +202,8 @@
     cols = width // 2
     term_2 = term_w(2).astype(BF)
     up_half, down_half = send(term_2[:, :cols], "y", 1), send(term_2[:, cols:], "y", 3)
+    core_a, core_b, left, term_2 = fence(core_a, core_b, left, term_2)
     term_1, term_3 = fence(term_w(1), term_w(3))
-    core_a, core_b, term_1, term_3 = fence(core_a, core_b, term_1, term_3)
 
     none = jnp.zeros_like(up_half)
     term_1 = term_1 + jnp.concatenate([up_half, none], 1).astype(F32)

time: 231 us -> 226 us (0.978)
  other arithmetic: 26.7 us -> 23.1 us
    ppermute x13, starting transfers between devices: 26.8 us -> 31.2 us  [send(): return lax.ppermute(a, axis, [(i, (i + k) % n) for i in range(n)])]
    ppermute x8, waiting for transfers between devices: 16.5 us -> 19.9 us  [exchange(): return lax.ppermute(a, axis, [(i, i ^ k) for i in range(4)])]
    ppermute x13, waiting for transfers between devices: 22.3 us -> 19.3 us  [send(): return lax.ppermute(a, axis, [(i, (i + k) % n) for i in range(n)])]
    ppermute x8, starting transfers between devices: 19 us -> 16.7 us  [exchange(): return lax.ppermute(a, axis, [(i, i ^ k) for i in range(4)])]
  transfers between devices with their start and end apart: 31 -> 31, of which waited for: 12 -> 14; matrix products, arithmetic and copies ran while one was open for 32% -> 30% of each run, Pallas kernels for 0% -> 0%
where the time goes in v1:
time: 226 us; the launch traced here: 225 us
  starting transfers between devices  72.1 us (32%)
  waiting for transfers between devices  64.5 us (29%)
  local copies, waits for them, and re-layouts  27.3 us (12%)
  matrix products  23.5 us (10%)
  other arithmetic  23.1 us (10%)
  between operations  14.5 us (6%)
    ppermute x13, starting transfers between devices, send(): return lax.ppermute(a, axis, [(i, (i + k) % n) for i in range(n)])  31.2 us
    ppermute x8, waiting for transfers between devices, exchange(): return lax.ppermute(a, axis, [(i, i ^ k) for i in range(4)])  19.9 us
    ppermute x13, waiting for transfers between devices, send(): return lax.ppermute(a, axis, [(i, (i + k) % n) for i in range(n)])  19.3 us
    ppermute x8, starting transfers between devices, exchange(): return lax.ppermute(a, axis, [(i, i ^ k) for i in range(4)])  16.7 us
    dot_general x5, matrix products, nn(): lax.dot_general(a, b, (((1,), (0,)), ((), ())), preferred_element_type=F32)  12.8 us
    ppermute x1, starting transfers between devices, on_device(): ends = lax.ppermute(ends, ('inp', 'h'), [(6, 1), (7, 0), (0, 7), (1, 6)])  10.6 us
    ppermute x1, waiting for transfers between devices, on_device(): last = lax.ppermute(far, 'inp', [(2, 3), (1, 0)])  7.86 us
    unnamed x64, local copies, waits for them, and re-layouts  6.36 us
  transfers between devices with their start and end apart: 31, of which 14 were waited for; matrix products, arithmetic and copies ran while one was open for 30% of the time, Pallas kernels for 0%

profile of v1, /device:TPU:1, one launch (start us, length us, event | category | flops | bytes accessed | tf_op | source)
XLA Modules:
  0.0 225.1 jit_solution(850698286252961514)
XLA Ops:
  9.7 7.7 %collective-permute-start = (bf16[128,1280]{1,0:T(8,128)(2,1)}, bf16[128,1280]{1,0:T(8,128)(2,1)}, u32[]{:S(2)}, u32[]{:S(2)}) collective-permute-start(bf16[128,1280]{1,0:T(8,128)(2,1)} %pad_maximum_fusion.12), channel_id=1, source_target_pairs={{0,1},{1,0},{2,3},{3,2},{4,5},{5,4},{6,7},{7,6},{8,9},{9,8},{10,11... | collective-permute-start | bytes 983048 | tf_op jit(solution)/shard_map/ppermute | solution.py:15
  19.2 6.5 %collective-permute-done = bf16[128,1280]{1,0:T(8,128)(2,1)} collective-permute-done((bf16[128,1280]{1,0:T(8,128)(2,1)}, bf16[128,1280]{1,0:T(8,128)(2,1)}, u32[]{:S(2)}, u32[]{:S(2)}) %collective-permute-start) | collective-permute-done | bytes 327712 | tf_op jit(solution)/shard_map/ppermute | solution.py:15
  29.4 2.5 %collective-permute-start.2 = (bf16[64,1280]{1,0:T(8,128)(2,1)S(1)}, bf16[64,1280]{1,0:T(8,128)(2,1)S(1)}, u32[]{:S(2)}, u32[]{:S(2)}) collective-permute-start(bf16[64,1280]{1,0:T(8,128)(2,1)S(1)} %get-tuple-element.79), channel_id=1, source_target_pairs={{0,32},{16,48},{32,0},{48,16},{1,33},{17,49},{33,1},{49,17},{2,34}... | collective-permute-start | bytes 491528 | tf_op jit(solution)/shard_map/ppermute | solution.py:15
  33.0 10.6 %collective-permute-start.5 = (bf16[4,160,512]{2,1,0:T(8,128)(2,1)S(1)}, bf16[4,160,512]{2,1,0:T(8,128)(2,1)}, u32[]{:S(2)}, u32[]{:S(2)}) collective-permute-start(bf16[4,160,512]{2,1,0:T(8,128)(2,1)S(1)} %get-tuple-element.158), channel_id=1, source_target_pairs={{192,1},{193,0},{0,193},{1,192},{194,3},{195,2},{2,195},{3,194},{1... | collective-permute-start | bytes 1966088 | tf_op jit(solution)/shard_map/ppermute | solution.py:103
  45.8 2.5 %dynamic-slice_bitcast_fusion.7 = (bf16[160,1280]{1,0:T(8,128)(2,1)}, bf16[160,1280]{1,0:T(8,128)(2,1)S(1)}, bf16[160,1280]{1,0:T(8,128)(2,1)S(1)}, bf16[160,1280]{1,0:T(8,128)(2,1)}) fusion(bf16[4,160,1280]{2,1,0:T(8,128)(2,1)} %bitcast.111, s32[]{:T(128)S(6)} %select_n.187, s32[]{:T(128)S(6)} %select_n.190, s32[]{:T(128)S(6)} %select_n.189, s32[]{:T(128)S(6)} %select_n.188), kind=kLoop, calls=%fused_computation.92 | loop fusion | bytes 3276816 | tf_op jit(solution)/shard_map/jit(dynamic_index_in_dim)/squeeze | solution.py:43
  57.3 2.6 %collective-permute-start.6 = (bf16[4,160,512]{2,1,0:T(8,128)(2,1)}, bf16[4,160,512]{2,1,0:T(8,128)(2,1)}, u32[]{:S(2)}, u32[]{:S(2)}) collective-permute-start(bf16[4,160,512]{2,1,0:T(8,128)(2,1)} %collective-permute-done.5), channel_id=1, source_target_pairs={{0,64},{192,128},{1,65},{193,129},{2,66},{194,130},{3,67},{195,131... | collective-permute-start | bytes 1966088 | tf_op jit(solution)/shard_map/ppermute | solution.py:127
  65.9 6.1 %collective-permute-done.6 = bf16[4,160,512]{2,1,0:T(8,128)(2,1)} collective-permute-done((bf16[4,160,512]{2,1,0:T(8,128)(2,1)}, bf16[4,160,512]{2,1,0:T(8,128)(2,1)}, u32[]{:S(2)}, u32[]{:S(2)}) %collective-permute-start.6) | collective-permute-done | bytes 655392 | tf_op jit(solution)/shard_map/ppermute | solution.py:127
  72.0 5.4 %collective-permute-start.8 = (bf16[160,512]{1,0:T(8,128)(2,1)}, bf16[160,512]{1,0:T(8,128)(2,1)S(1)}, u32[]{:S(2)}, u32[]{:S(2)}) collective-permute-start(bf16[160,512]{1,0:T(8,128)(2,1)} %slice.104), channel_id=1, source_target_pairs={{0,128},{64,192},{128,0},{192,64},{1,129},{65,193},{129,1},{193,65... | collective-permute-start | bytes 491528 | tf_op jit(solution)/shard_map/ppermute | solution.py:72
  84.7 4.8 %collective-permute-done.9 = bf16[320,512]{1,0:T(8,128)(2,1)} collective-permute-done((bf16[320,512]{1,0:T(8,128)(2,1)}, bf16[320,512]{1,0:T(8,128)(2,1)}, u32[]{:S(2)}, u32[]{:S(2)}) %collective-permute-start.9) | collective-permute-done | bytes 327712 | tf_op jit(solution)/shard_map/ppermute | solution.py:72
  90.6 8.7 %collective-permute-start.12 = (bf16[160,512]{1,0:T(8,128)(2,1)S(1)}, bf16[160,512]{1,0:T(8,128)(2,1)S(1)}, u32[]{:S(2)}, u32[]{:S(2)}) collective-permute-start(bf16[160,512]{1,0:T(8,128)(2,1)S(1)} %slice.103), channel_id=1, source_target_pairs={{0,128},{64,192},{128,0},{192,64},{1,129},{65,193},{129,1},{193,65... | collective-permute-start | bytes 491528 | tf_op jit(solution)/shard_map/ppermute | solution.py:72
  101.9 11.1 %collective-permute-done.11 = bf16[160,512]{1,0:T(8,128)(2,1)S(1)} collective-permute-done((bf16[160,512]{1,0:T(8,128)(2,1)S(1)}, bf16[160,512]{1,0:T(8,128)(2,1)S(1)}, u32[]{:S(2)}, u32[]{:S(2)}) %collective-permute-start.11) | collective-permute-done | bytes 163872 | tf_op jit(solution)/shard_map/ppermute | solution.py:72
  113.1 7.9 %collective-permute-done.13 = bf16[4,160,512]{2,1,0:T(8,128)(2,1)S(1)} collective-permute-done((bf16[4,160,512]{2,1,0:T(8,128)(2,1)}, bf16[4,160,512]{2,1,0:T(8,128)(2,1)S(1)}, u32[]{:S(2)}, u32[]{:S(2)}) %collective-permute-start.13) | collective-permute-done | bytes 655392 | tf_op jit(solution)/shard_map/ppermute | solution.py:144
  121.2 2.1 collective-permute-start.14
  123.3 2.5 %constant_dynamic-update-slice_fusion.2 = bf16[1024,1280]{1,0:T(8,128)(2,1)} fusion(bf16[1024,1280]{1,0:T(8,128)(2,1)} %constant_dynamic-update-slice_fusion.3, bf16[512,1280]{1,0:T(8,128)(2,1)} %all-gather.5.cloned.1.call-done), kind=kLoop, calls=%fused_computation.107 | loop fusion | bytes 2621440 | tf_op jit(solution)/shard_map/concatenate | solution.py:197
  125.8 2.6 %fusion.6 = (bf16[4,160,512]{2,1,0:T(8,128)(2,1)S(1)}, bf16[4,160,512]{2,1,0:T(8,128)(2,1)S(1)}, bf16[4,160,512]{2,1,0:T(8,128)(2,1)S(1)}) fusion(bf16[4,160,512]{2,1,0:T(8,128)(2,1)} %collective-permute-done.5, bf16[4,160,512]{2,1,0:T(8,128)(2,1)} %collective-permute-done.6, bf16[4,160,512]{2,1,0:T(8,128)(2,1)} %collective-permute-done.10, ...), kind=kLoop, calls=%fused_computation.29 | loop fusion | flops 4587520 | bytes 4587524 | tf_op jit(solution)/shard_map/convert_element_type | solution.py:158
  128.5 3.1 %convolution_convert_fusion = bf16[640,1280]{1,0:T(8,128)(2,1)} fusion(bf16[512,1280]{1,0:T(8,128)(2,1)S(1)} %copy-done.5, bf16[512,1280]{1,0:T(8,128)(2,1)S(1)} %copy-done.29, bf16[640,512]{1,0:T(8,128)(2,1)S(1)} %bitcast.113, bf16[640,512]{1,0:T(8,128)(2,1)S(1)} %bitcast.112), kind=kOutput, calls=%fused_computation.2 | convolution fusion | flops 1686405120 | bytes 5570560 | tf_op jit(solution)/shard_map/dot_general | solution.py:31
  135.8 3.9 %fusion.61 = f32[512,1280]{1,0:T(8,128)S(1)} fusion(bf16[1280,512]{1,0:T(8,128)(2,1)S(1)} %bitcast.101, bf16[1280,1280]{1,0:T(8,128)(2,1)} %all-gather.7.cloned.1.call-done), kind=kOutput, calls=%fused_computation.136 | convolution fusion | flops 1677721600 | bytes 7208960 | tf_op jit(solution)/shard_map/dot_general | solution.py:35
  139.6 3.0 %collective-permute-done.16 = bf16[320,512]{1,0:T(8,128)(2,1)} collective-permute-done((bf16[320,512]{1,0:T(8,128)(2,1)S(1)}, bf16[320,512]{1,0:T(8,128)(2,1)}, u32[]{:S(2)}, u32[]{:S(2)}) %collective-permute-start.16) | collective-permute-done | bytes 327712 | tf_op jit(solution)/shard_map/ppermute | solution.py:72
  148.6 3.6 %collective-permute-start.17 = (f32[256,1280]{1,0:T(8,128)S(1)}, f32[256,1280]{1,0:T(8,128)S(1)}, u32[]{:S(2)}, u32[]{:S(2)}) collective-permute-start(f32[256,1280]{1,0:T(8,128)S(1)} %constant_dynamic-slice_fusion.1), channel_id=1, source_target_pairs={{0,8},{8,0},{1,9},{9,1},{2,10},{10,2},{3,11},{11,3},{4,12},{12,4},... | collective-permute-start | bytes 3932168 | tf_op jit(solution)/shard_map/ppermute | solution.py:15
  155.9 2.9 %collective-permute-start.22 = (bf16[320,640]{1,0:T(8,128)(2,1)S(1)}, bf16[320,640]{1,0:T(8,128)(2,1)}, u32[]{:S(2)}, u32[]{:S(2)}) collective-permute-start(bf16[320,640]{1,0:T(8,128)(2,1)S(1)} %get-tuple-element.140), channel_id=1, source_target_pairs={{0,6},{2,0},{4,2},{6,4},{1,7},{3,1},{5,3},{7,5},{8,14},{10,8},{12,... | collective-permute-start | bytes 1228808 | tf_op jit(solution)/shard_map/ppermute | solution.py:15
  160.3 4.3 %all-to-all-start = ((bf16[4,2,64,1280]{3,2,1,0:T(8,128)(2,1)}), bf16[4,2,64,1280]{3,2,1,0:T(8,128)(2,1)}, u32[]{:S(2)}, u32[]{:S(2)}) async-start(bf16[4,2,64,1280]{3,2,1,0:T(8,128)(2,1)} %fusion.1), calls=%async_computation | async-start | bytes 2621440 | tf_op jit(solution)/shard_map/all_to_all | solution.py:213
  164.7 3.1 %fusion.34 = f32[320,1280]{1,0:T(8,128)S(1)} fusion(bf16[1024,1280]{1,0:T(8,128)(2,1)} %constant_dynamic-update-slice_fusion.2, bf16[1280,1024]{1,0:T(8,128)(2,1)} %copy-done.8, s32[]{:T(128)S(6)} %select_n.227), kind=kOutput, calls=%fused_computation.71 | convolution fusion | flops 838860800 | bytes 4915204 | tf_op jit(solution)/shard_map/dot_general | solution.py:31
  167.8 2.1 fusion.36
  173.7 2.5 %collective-permute-start.23 = (bf16[320,1280]{1,0:T(8,128)(2,1)}, bf16[320,1280]{1,0:T(8,128)(2,1)}, u32[]{:S(2)}, u32[]{:S(2)}) collective-permute-start(bf16[320,1280]{1,0:T(8,128)(2,1)} %add_convert_fusion), channel_id=1, source_target_pairs={{0,6},{2,0},{4,2},{6,4},{1,7},{3,1},{5,3},{7,5},{8,14},{10,8},{12,... | collective-permute-start | bytes 2457608 | tf_op jit(solution)/shard_map/ppermute | solution.py:15
  178.2 3.7 %all-to-all-done = bf16[4,2,64,1280]{3,2,1,0:T(8,128)(2,1)} async-done(((bf16[4,2,64,1280]{3,2,1,0:T(8,128)(2,1)}), bf16[4,2,64,1280]{3,2,1,0:T(8,128)(2,1)}, u32[]{:S(2)}, u32[]{:S(2)}) %all-to-all-start) | async-done | bytes 1310752 | tf_op jit(solution)/shard_map/all_to_all | solution.py:213
  183.8 3.8 %collective-permute-start.19 = (bf16[64,1280]{1,0:T(8,128)(2,1)S(1)}, bf16[64,1280]{1,0:T(8,128)(2,1)S(1)}, u32[]{:S(2)}, u32[]{:S(2)}) collective-permute-start(bf16[64,1280]{1,0:T(8,128)(2,1)S(1)} %fusion.45), channel_id=1, source_target_pairs={{0,1},{1,0},{2,3},{3,2},{4,5},{5,4},{6,7},{7,6},{8,9},{9,8},{10,11... | collective-permute-start | bytes 491528 | tf_op jit(solution)/shard_map/ppermute | solution.py:15
  187.6 5.8 %collective-permute-done.23 = bf16[320,1280]{1,0:T(8,128)(2,1)} collective-permute-done((bf16[320,1280]{1,0:T(8,128)(2,1)}, bf16[320,1280]{1,0:T(8,128)(2,1)}, u32[]{:S(2)}, u32[]{:S(2)}) %collective-permute-start.23) | collective-permute-done | bytes 819232 | tf_op jit(solution)/shard_map/ppermute | solution.py:15
  193.5 5.1 %collective-permute-done.21 = bf16[320,1280]{1,0:T(8,128)(2,1)} collective-permute-done((bf16[320,1280]{1,0:T(8,128)(2,1)}, bf16[320,1280]{1,0:T(8,128)(2,1)}, u32[]{:S(2)}, u32[]{:S(2)}) %collective-permute-start.21) | collective-permute-done | bytes 819232 | tf_op jit(solution)/shard_map/ppermute | solution.py:15
  199.5 3.8 %all-to-all-start.1 = ((bf16[4,64,1280]{2,1,0:T(8,128)(2,1)}), bf16[4,64,1280]{2,1,0:T(8,128)(2,1)S(1)}, u32[]{:S(2)}, u32[]{:S(2)}) async-start(bf16[4,64,1280]{2,1,0:T(8,128)(2,1)} %tile.2), calls=%async_computation.2 | async-start | bytes 1310720 | tf_op jit(solution)/shard_map/all_to_all | solution.py:39
  203.3 3.4 %fusion = f32[320,1280]{1,0:T(8,128)S(1)} fusion(bf16[1024,1280]{1,0:T(8,128)(2,1)} %constant_dynamic-update-slice_fusion.2, bf16[320,1280]{1,0:T(8,128)(2,1)} %collective-permute-done.23, bf16[320,1280]{1,0:T(8,128)(2,1)} %collective-permute-done.21, bf16[1280,1024]{1,0:T(8,128)(2,1)} %copy-done.8, s32[]{:T(128)S(6)} %select_n.229), kind=kOutput, calls=%fused_computation.7 | convolution fusion | flops 840499200 | bytes 6553604 | tf_op jit(solution)/shard_map/dot_general | solution.py:31
  206.7 5.0 %all-to-all-done.1 = bf16[4,64,1280]{2,1,0:T(8,128)(2,1)S(1)} async-done(((bf16[4,64,1280]{2,1,0:T(8,128)(2,1)}), bf16[4,64,1280]{2,1,0:T(8,128)(2,1)S(1)}, u32[]{:S(2)}, u32[]{:S(2)}) %all-to-all-start.1) | async-done | bytes 655392 | tf_op jit(solution)/shard_map/all_to_all | solution.py:39
  211.7 3.4 %collective-permute-start.24 = (bf16[256,1280]{1,0:T(8,128)(2,1)S(1)}, bf16[256,1280]{1,0:T(8,128)(2,1)S(1)}, u32[]{:S(2)}, u32[]{:S(2)}) collective-permute-start(bf16[256,1280]{1,0:T(8,128)(2,1)S(1)} %bitcast.109), channel_id=1, source_target_pairs={{0,8},{8,0},{1,9},{9,1},{2,10},{10,2},{3,11},{11,3},{4,12},{12,4},... | collective-permute-start | bytes 1966088 | tf_op jit(solution)/shard_map/ppermute | solution.py:15
  (178 shorter events, 66.1 us)
Async XLA Ops:
  7.2 38.6 %all-gather.9.cloned.1.call-start = ((), (), s32[]{:S(2)}) async-start(), calls=%async_computation.6 | async-start | bytes 2048000 | tf_op jit(solution)/shard_map/all_gather | solution.py:95
  7.9 105.2 %all-gather.5.cloned.1.call-start = ((), (), s32[]{:S(2)}) async-start(), calls=%async_computation.3 | async-start | bytes 1474560 | tf_op jit(solution)/shard_map/all_gather | solution.py:109
  9.7 15.9 %collective-permute-start = (bf16[128,1280]{1,0:T(8,128)(2,1)}, bf16[128,1280]{1,0:T(8,128)(2,1)}, u32[]{:S(2)}, u32[]{:S(2)}) collective-permute-start(bf16[128,1280]{1,0:T(8,128)(2,1)} %pad_maximum_fusion.12), channel_id=1, source_target_pairs={{0,1},{1,0},{2,3},{3,2},{4,5},{5,4},{6,7},{7,6},{8,9},{9,8},{10,11... | collective-permute-start | bytes 983048 | tf_op jit(solution)/shard_map/ppermute | solution.py:15
  27.4 108.4 %all-gather.7.cloned.1.call-start = ((), (), s32[]{:S(2)}) async-start(), calls=%async_computation.4 | async-start | bytes 4096000 | tf_op jit(solution)/shard_map/all_gather | solution.py:108
  27.6 18.1 %collective-permute-start.3 = (bf16[64,1280]{1,0:T(8,128)(2,1)S(1)}, bf16[64,1280]{1,0:T(8,128)(2,1)S(1)}, u32[]{:S(2)}, u32[]{:S(2)}) collective-permute-start(bf16[64,1280]{1,0:T(8,128)(2,1)S(1)} %get-tuple-element.79), channel_id=1, source_target_pairs={{0,16},{16,32},{32,48},{48,0},{1,17},{17,33},{33,49},{49,1},{2,18}... | collective-permute-start | bytes 491528 | tf_op jit(solution)/shard_map/ppermute | solution.py:15
  29.4 16.3 %collective-permute-start.2 = (bf16[64,1280]{1,0:T(8,128)(2,1)S(1)}, bf16[64,1280]{1,0:T(8,128)(2,1)S(1)}, u32[]{:S(2)}, u32[]{:S(2)}) collective-permute-start(bf16[64,1280]{1,0:T(8,128)(2,1)S(1)} %get-tuple-element.79), channel_id=1, source_target_pairs={{0,32},{16,48},{32,0},{48,16},{1,33},{17,49},{33,1},{49,17},{2,34}... | collective-permute-start | bytes 491528 | tf_op jit(solution)/shard_map/ppermute | solution.py:15
  31.8 13.9 %collective-permute-start.1 = (bf16[64,1280]{1,0:T(8,128)(2,1)S(1)}, bf16[64,1280]{1,0:T(8,128)(2,1)S(1)}, u32[]{:S(2)}, u32[]{:S(2)}) collective-permute-start(bf16[64,1280]{1,0:T(8,128)(2,1)S(1)} %get-tuple-element.79), channel_id=1, source_target_pairs={{0,48},{16,0},{32,16},{48,32},{1,49},{17,1},{33,17},{49,33},{2,50}... | collective-permute-start | bytes 491528 | tf_op jit(solution)/shard_map/ppermute | solution.py:15
  33.0 24.3 %collective-permute-start.5 = (bf16[4,160,512]{2,1,0:T(8,128)(2,1)S(1)}, bf16[4,160,512]{2,1,0:T(8,128)(2,1)}, u32[]{:S(2)}, u32[]{:S(2)}) collective-permute-start(bf16[4,160,512]{2,1,0:T(8,128)(2,1)S(1)} %get-tuple-element.158), channel_id=1, source_target_pairs={{192,1},{193,0},{0,193},{1,192},{194,3},{195,2},{2,195},{3,194},{1... | collective-permute-start | bytes 1966088 | tf_op jit(solution)/shard_map/ppermute | solution.py:103
  50.6 9.6 %collective-permute-start.4 = (bf16[320,512]{1,0:T(8,128)(2,1)}, bf16[320,512]{1,0:T(8,128)(2,1)}, u32[]{:S(2)}, u32[]{:S(2)}) collective-permute-start(bf16[320,512]{1,0:T(8,128)(2,1)} %convolution_convert_fusion.3), channel_id=1, source_target_pairs={{0,64},{64,0},{128,192},{192,128},{1,65},{65,1},{129,193},{193,129... | collective-permute-start | bytes 983048 | tf_op jit(solution)/shard_map/ppermute | solution.py:72
  51.7 10.9 %collective-permute-start.7 = (bf16[4,64,1280]{2,1,0:T(8,128)(2,1)}, bf16[4,64,1280]{2,1,0:T(8,128)(2,1)}, u32[]{:S(2)}, u32[]{:S(2)}) collective-permute-start(bf16[4,64,1280]{2,1,0:T(8,128)(2,1)} %select_select_fusion.4), channel_id=1, source_target_pairs={{0,8},{8,0},{1,9},{9,1},{2,10},{10,2},{3,11},{11,3},{4,12},{12,4},... | collective-permute-start | bytes 1966088 | tf_op jit(solution)/shard_map/ppermute | solution.py:15
  54.0 133.6 %reduce-scatter.2.cloned.1.call-start = ((), (), s32[]{:S(2)}) async-start(), calls=%async_computation.5 | async-start | bytes 2048000 | tf_op jit(solution)/shard_map/reduce_scatter | solution.py:181
  57.3 14.7 %collective-permute-start.6 = (bf16[4,160,512]{2,1,0:T(8,128)(2,1)}, bf16[4,160,512]{2,1,0:T(8,128)(2,1)}, u32[]{:S(2)}, u32[]{:S(2)}) collective-permute-start(bf16[4,160,512]{2,1,0:T(8,128)(2,1)} %collective-permute-done.5), channel_id=1, source_target_pairs={{0,64},{192,128},{1,65},{193,129},{2,66},{194,130},{3,67},{195,131... | collective-permute-start | bytes 1966088 | tf_op jit(solution)/shard_map/ppermute | solution.py:127
  72.0 12.7 %collective-permute-start.8 = (bf16[160,512]{1,0:T(8,128)(2,1)}, bf16[160,512]{1,0:T(8,128)(2,1)S(1)}, u32[]{:S(2)}, u32[]{:S(2)}) collective-permute-start(bf16[160,512]{1,0:T(8,128)(2,1)} %slice.104), channel_id=1, source_target_pairs={{0,128},{64,192},{128,0},{192,64},{1,129},{65,193},{129,1},{193,65... | collective-permute-start | bytes 491528 | tf_op jit(solution)/shard_map/ppermute | solution.py:72
  77.4 12.0 %collective-permute-start.9 = (bf16[320,512]{1,0:T(8,128)(2,1)}, bf16[320,512]{1,0:T(8,128)(2,1)}, u32[]{:S(2)}, u32[]{:S(2)}) collective-permute-start(bf16[320,512]{1,0:T(8,128)(2,1)} %convolution_convert_fusion.2), channel_id=1, source_target_pairs={{0,64},{64,0},{128,192},{192,128},{1,65},{65,1},{129,193},{193,129... | collective-permute-start | bytes 983048 | tf_op jit(solution)/shard_map/ppermute | solution.py:72
  77.5 13.1 %collective-permute-start.10 = (bf16[4,160,512]{2,1,0:T(8,128)(2,1)}, bf16[4,160,512]{2,1,0:T(8,128)(2,1)}, u32[]{:S(2)}, u32[]{:S(2)}) collective-permute-start(bf16[4,160,512]{2,1,0:T(8,128)(2,1)} %collective-permute-done.6), channel_id=1, source_target_pairs={{64,128},{128,64},{65,129},{129,65},{66,130},{130,66},{67,131},{13... | collective-permute-start | bytes 1966088 | tf_op jit(solution)/shard_map/ppermute | solution.py:136
  90.6 22.5 %collective-permute-start.12 = (bf16[160,512]{1,0:T(8,128)(2,1)S(1)}, bf16[160,512]{1,0:T(8,128)(2,1)S(1)}, u32[]{:S(2)}, u32[]{:S(2)}) collective-permute-start(bf16[160,512]{1,0:T(8,128)(2,1)S(1)} %slice.103), channel_id=1, source_target_pairs={{0,128},{64,192},{128,0},{192,64},{1,129},{65,193},{129,1},{193,65... | collective-permute-start | bytes 491528 | tf_op jit(solution)/shard_map/ppermute | solution.py:72
  99.3 13.7 %collective-permute-start.11 = (bf16[160,512]{1,0:T(8,128)(2,1)S(1)}, bf16[160,512]{1,0:T(8,128)(2,1)S(1)}, u32[]{:S(2)}, u32[]{:S(2)}) collective-permute-start(bf16[160,512]{1,0:T(8,128)(2,1)S(1)} %add_convert_fusion.3), channel_id=1, source_target_pairs={{0,128},{64,192},{128,0},{192,64},{1,129},{65,193},{129,1},{193,65... | collective-permute-start | bytes 491528 | tf_op jit(solution)/shard_map/ppermute | solution.py:72
  99.4 21.6 %collective-permute-start.13 = (bf16[4,160,512]{2,1,0:T(8,128)(2,1)}, bf16[4,160,512]{2,1,0:T(8,128)(2,1)S(1)}, u32[]{:S(2)}, u32[]{:S(2)}) collective-permute-start(bf16[4,160,512]{2,1,0:T(8,128)(2,1)} %collective-permute-done.10), channel_id=1, source_target_pairs={{128,192},{64,0},{129,193},{65,1},{130,194},{66,2},{131,195},{67,3... | collective-permute-start | bytes 1966088 | tf_op jit(solution)/shard_map/ppermute | solution.py:144
  121.0 10.6 %collective-permute-start.15 = (bf16[160,512]{1,0:T(8,128)(2,1)S(1)}, bf16[160,512]{1,0:T(8,128)(2,1)}, u32[]{:S(2)}, u32[]{:S(2)}) collective-permute-start(bf16[160,512]{1,0:T(8,128)(2,1)S(1)} %add_convert_fusion.2), channel_id=1, source_target_pairs={{0,128},{64,192},{128,0},{192,64},{1,129},{65,193},{129,1},{193,65... | collective-permute-start | bytes 491528 | tf_op jit(solution)/shard_map/ppermute | solution.py:72
  121.2 12.2 %collective-permute-start.14 = (bf16[320,512]{1,0:T(8,128)(2,1)S(1)}, bf16[320,512]{1,0:T(8,128)(2,1)}, u32[]{:S(2)}, u32[]{:S(2)}) collective-permute-start(bf16[320,512]{1,0:T(8,128)(2,1)S(1)} %pad_maximum_fusion.13), channel_id=1, source_target_pairs={{0,64},{64,0},{128,192},{192,128},{1,65},{65,1},{129,193},{193,129... | collective-permute-start | bytes 983048 | tf_op jit(solution)/shard_map/ppermute | solution.py:72
  135.6 7.1 %collective-permute-start.16 = (bf16[320,512]{1,0:T(8,128)(2,1)S(1)}, bf16[320,512]{1,0:T(8,128)(2,1)}, u32[]{:S(2)}, u32[]{:S(2)}) collective-permute-start(bf16[320,512]{1,0:T(8,128)(2,1)S(1)} %pad_maximum_fusion.14), channel_id=1, source_target_pairs={{0,64},{64,0},{128,192},{192,128},{1,65},{65,1},{129,193},{193,129... | collective-permute-start | bytes 983048 | tf_op jit(solution)/shard_map/ppermute | solution.py:72
  148.6 10.3 %collective-permute-start.17 = (f32[256,1280]{1,0:T(8,128)S(1)}, f32[256,1280]{1,0:T(8,128)S(1)}, u32[]{:S(2)}, u32[]{:S(2)}) collective-permute-start(f32[256,1280]{1,0:T(8,128)S(1)} %constant_dynamic-slice_fusion.1), channel_id=1, source_target_pairs={{0,8},{8,0},{1,9},{9,1},{2,10},{10,2},{3,11},{11,3},{4,12},{12,4},... | collective-permute-start | bytes 3932168 | tf_op jit(solution)/shard_map/ppermute | solution.py:15
  152.3 6.7 %collective-permute-start.18 = (f32[256,1280]{1,0:T(8,128)S(1)}, f32[256,1280]{1,0:T(8,128)S(1)}, u32[]{:S(2)}, u32[]{:S(2)}) collective-permute-start(f32[256,1280]{1,0:T(8,128)S(1)} %constant_dynamic-slice_fusion), channel_id=1, source_target_pairs={{0,8},{8,0},{1,9},{9,1},{2,10},{10,2},{3,11},{11,3},{4,12},{12,4},... | collective-permute-start | bytes 3932168 | tf_op jit(solution)/shard_map/ppermute | solution.py:15
  155.9 15.8 %collective-permute-start.22 = (bf16[320,640]{1,0:T(8,128)(2,1)S(1)}, bf16[320,640]{1,0:T(8,128)(2,1)}, u32[]{:S(2)}, u32[]{:S(2)}) collective-permute-start(bf16[320,640]{1,0:T(8,128)(2,1)S(1)} %get-tuple-element.140), channel_id=1, source_target_pairs={{0,6},{2,0},{4,2},{6,4},{1,7},{3,1},{5,3},{7,5},{8,14},{10,8},{12,... | collective-permute-start | bytes 1228808 | tf_op jit(solution)/shard_map/ppermute | solution.py:15
  158.8 17.4 %collective-permute-start.20 = (bf16[320,640]{1,0:T(8,128)(2,1)S(1)}, bf16[320,640]{1,0:T(8,128)(2,1)}, u32[]{:S(2)}, u32[]{:S(2)}) collective-permute-start(bf16[320,640]{1,0:T(8,128)(2,1)S(1)} %get-tuple-element.141), channel_id=1, source_target_pairs={{0,2},{2,4},{4,6},{6,0},{1,3},{3,5},{5,7},{7,1},{8,10},{10,12},{12... | collective-permute-start | bytes 1228808 | tf_op jit(solution)/shard_map/ppermute | solution.py:15
  160.3 21.6 %all-to-all-start = ((bf16[4,2,64,1280]{3,2,1,0:T(8,128)(2,1)}), bf16[4,2,64,1280]{3,2,1,0:T(8,128)(2,1)}, u32[]{:S(2)}, u32[]{:S(2)}) async-start(bf16[4,2,64,1280]{3,2,1,0:T(8,128)(2,1)} %fusion.1), calls=%async_computation | async-start | bytes 2621440 | tf_op jit(solution)/shard_map/all_to_all | solution.py:213
  173.7 19.7 %collective-permute-start.23 = (bf16[320,1280]{1,0:T(8,128)(2,1)}, bf16[320,1280]{1,0:T(8,128)(2,1)}, u32[]{:S(2)}, u32[]{:S(2)}) collective-permute-start(bf16[320,1280]{1,0:T(8,128)(2,1)} %add_convert_fusion), channel_id=1, source_target_pairs={{0,6},{2,0},{4,2},{6,4},{1,7},{3,1},{5,3},{7,5},{8,14},{10,8},{12,... | collective-permute-start | bytes 2457608 | tf_op jit(solution)/shard_map/ppermute | solution.py:15
  178.2 20.3 %collective-permute-start.21 = (bf16[320,1280]{1,0:T(8,128)(2,1)}, bf16[320,1280]{1,0:T(8,128)(2,1)}, u32[]{:S(2)}, u32[]{:S(2)}) collective-permute-start(bf16[320,1280]{1,0:T(8,128)(2,1)} %add_convert_fusion.1), channel_id=1, source_target_pairs={{0,2},{2,4},{4,6},{6,0},{1,3},{3,5},{5,7},{7,1},{8,10},{10,12},{12... | collective-permute-start | bytes 2457608 | tf_op jit(solution)/shard_map/ppermute | solution.py:15
  183.8 14.8 %collective-permute-start.19 = (bf16[64,1280]{1,0:T(8,128)(2,1)S(1)}, bf16[64,1280]{1,0:T(8,128)(2,1)S(1)}, u32[]{:S(2)}, u32[]{:S(2)}) collective-permute-start(bf16[64,1280]{1,0:T(8,128)(2,1)S(1)} %fusion.45), channel_id=1, source_target_pairs={{0,1},{1,0},{2,3},{3,2},{4,5},{5,4},{6,7},{7,6},{8,9},{9,8},{10,11... | collective-permute-start | bytes 491528 | tf_op jit(solution)/shard_map/ppermute | solution.py:15
  199.5 12.2 %all-to-all-start.1 = ((bf16[4,64,1280]{2,1,0:T(8,128)(2,1)}), bf16[4,64,1280]{2,1,0:T(8,128)(2,1)S(1)}, u32[]{:S(2)}, u32[]{:S(2)}) async-start(bf16[4,64,1280]{2,1,0:T(8,128)(2,1)} %tile.2), calls=%async_computation.2 | async-start | bytes 1310720 | tf_op jit(solution)/shard_map/all_to_all | solution.py:39
  203.3 11.8 %copy-start.20 = (bf16[160,1280]{1,0:T(8,128)(2,1)S(1)}, bf16[160,1280]{1,0:T(8,128)(2,1)}, u32[]{:S(2)}) copy-start(bf16[160,1280]{1,0:T(8,128)(2,1)} %reduce-scatter.2.cloned.1.call-done) | copy-start | bytes 1228804
  211.7 5.7 %collective-permute-start.24 = (bf16[256,1280]{1,0:T(8,128)(2,1)S(1)}, bf16[256,1280]{1,0:T(8,128)(2,1)S(1)}, u32[]{:S(2)}, u32[]{:S(2)}) collective-permute-start(bf16[256,1280]{1,0:T(8,128)(2,1)S(1)} %bitcast.109), channel_id=1, source_target_pairs={{0,8},{8,0},{1,9},{9,1},{2,10},{10,2},{3,11},{11,3},{4,12},{12,4},... | collective-permute-start | bytes 1966088 | tf_op jit(solution)/shard_map/ppermute | solution.py:15
  (31 other events, 91.6 us)
Sparse Core Ops, SparseCore 0:
  9.8 33.4 all-gather.8
  45.1 26.9 all-gather.4
  74.5 42.7 all-gather.6
  135.9 31.1 reduce-scatter.1
